TPU v7x, 256 devices: a whole 4x4x8 slice. The times are simulated.
256 devices in a mesh: seq: 32 (over z, y), mp: 8 (over x, core).
Axes of the slice: x: 4, y: 4, z: 8, core: 2. Of those that a mesh axis runs over, the one named last changes fastest.
Arguments:
- x_in: float32 [16384, 8192], P('seq', 'mp'), may hold values from -6 to 6
- dy_out: float32 [16384, 8192], P('seq', 'mp'), may hold values from -3 to 3
- b_in: float32 [16384, 128], P('seq'), may hold values from -0.18 to 0.18
- c_in: float32 [16384, 128], P('seq'), may hold values from -0.18 to 0.18
- log_decay: float32 [128, 16384], P('mp', 'seq'), may hold values from -1 to 0
- parents: int32 [32], replicated, may hold values from -1 to 30, as said below
- lengths: int32 [32], replicated, may hold values from 128 to 512, as said below
Outputs:
- x_grad: float32 [16384, 8192], P('seq', 'mp')
- b_grad: float32 [16384, 128], P('seq')
- c_grad: float32 [16384, 128], P('seq')
- decay_grad: float32 [128, 16384], P('mp', 'seq')
Inputs may be any that keep to these rules, and one draw needn't show every extreme that they name: parents[b] is an earlier block for every block b after the first; block 0 has none; the last block resumes from the block just before it. `lengths`: some block is full in every draw.
All inputs are finite; a program needn't handle non-finite values.
Results may differ from a plain program's by a relative error of at most 0.004.
Values may be sent and summed in bfloat16 or wider, within the bound.
A program may use at most 128 MiB of HBM per device.

v0:
```python
import jax
import jax.numpy as jnp
from jax import lax
from jax.sharding import PartitionSpec as P

highest = lax.Precision.HIGHEST


def chain_weights(decays, parents, count):
    blocks = jnp.arange(count, dtype=jnp.int32)
    width_heads = decays.shape[1]

    def step(k, state):
        weights, coef, ancestor = state
        match = ancestor[:, None] == blocks[None, :]
        onehot = match.astype(jnp.float32)
        weights = weights + onehot[:, :, None] * coef[:, None, :]
        coef = coef * jnp.dot(onehot, decays, precision=highest)
        upward = jnp.sum(jnp.where(match, parents[None, :], 0), axis=1)
        ancestor = jnp.where(ancestor >= 0, upward, -1)
        return (weights, coef, ancestor)

    init = (
        jnp.zeros((count, count, width_heads), jnp.float32),
        jnp.ones((count, width_heads), jnp.float32),
        parents,
    )
    weights, _, _ = lax.fori_loop(0, count, step, init)
    return weights


def local_states(x_blk, dy_blk, bmat, cmat, logd, length):
    rows = x_blk.shape[0]
    heads = logd.shape[0]
    width = x_blk.shape[1] // heads
    live = (jnp.arange(rows, dtype=jnp.int32) < length).astype(jnp.float32)
    xmask = x_blk * live[:, None]
    dymask = dy_blk * live[:, None]
    cumul = jnp.cumsum(logd * live[None, :], axis=1)
    last = cumul[:, -1]
    e_end = jnp.exp(last[:, None] - cumul)
    e_start = jnp.exp(cumul)
    xheads = xmask.reshape(rows, heads, width)
    dyheads = dymask.reshape(rows, heads, width)
    loc_end = jnp.einsum("tn,ht,thp->hnp", bmat, e_end, xheads, precision=highest)
    loc_adj = jnp.einsum("tn,ht,thp->hnp", cmat, e_start, dyheads, precision=highest)
    saved = (live, xheads, dyheads, cumul, e_end, e_start)
    return (jnp.exp(last), loc_end.astype(jnp.bfloat16), loc_adj.astype(jnp.bfloat16), saved)


def block_grads(bmat, cmat, saved, decay_tot, s_in, g_out):
    live, xheads, dyheads, cumul, e_end, e_start = saved
    rows = xheads.shape[0]
    heads = xheads.shape[1]
    scores = jnp.dot(cmat, bmat.T, precision=highest)
    steps = jnp.arange(rows, dtype=jnp.int32)
    lower = steps[:, None] >= steps[None, :]
    final = (steps == rows - 1).astype(jnp.float32)

    def one_head(carry, item):
        db_sum, dc_sum = carry
        xk, dk, ck, ee, es, dk_dec, hk, gk = item
        diff = jnp.where(lower, ck[:, None] - ck[None, :], 0.0)
        decay = jnp.where(lower, jnp.exp(diff), 0.0)
        pairs = jnp.dot(dk, xk.T, precision=highest)
        dsc = decay * scores
        dpr = decay * pairs
        joint = dsc * pairs
        bgo = jnp.dot(bmat, gk, precision=highest)
        chi = jnp.dot(cmat, hk, precision=highest)
        dx_head = (jnp.dot(dsc.T, dk, precision=highest) + ee[:, None] * bgo) * live[:, None]
        db_head = jnp.dot(dpr.T, cmat, precision=highest) + ee[:, None] * jnp.dot(
            xk, gk.T, precision=highest
        )
        dc_head = jnp.dot(dpr, bmat, precision=highest) + es[:, None] * jnp.dot(
            dk, hk.T, precision=highest
        )
        tail = ee * jnp.sum(bgo * xk, axis=1)
        extra = jnp.sum(tail) + dk_dec * jnp.sum(gk * hk)
        dcum = (
            jnp.sum(joint, axis=1)
            - jnp.sum(joint, axis=0)
            + es * jnp.sum(chi * dk, axis=1)
            - tail
            + final * extra
        )
        dlog = jnp.cumsum(dcum[::-1])[::-1] * live
        return ((db_sum + db_head, dc_sum + dc_head), (dx_head, dlog))

    zero_n = jnp.zeros((rows, bmat.shape[1]), jnp.float32)
    items = (
        xheads.transpose(1, 0, 2),
        dyheads.transpose(1, 0, 2),
        cumul,
        e_end,
        e_start,
        decay_tot,
        s_in,
        g_out,
    )
    (db_sum, dc_sum), (dx_all, dlog_all) = lax.scan(one_head, (zero_n, zero_n), items)
    dx = dx_all.transpose(1, 0, 2).reshape(rows, heads * xheads.shape[2])
    return (dx, db_sum, dc_sum, dlog_all)


def on_device(x_in, dy_out, b_in, c_in, log_decay, parents, lengths):
    count = lax.axis_size("seq")
    mine = lax.axis_index("seq")
    blocks = jnp.arange(count, dtype=jnp.int32)
    length = jnp.sum(jnp.where(blocks == mine, lengths, 0))
    decay_tot, loc_end, loc_adj, saved = local_states(x_in, dy_out, b_in, c_in, log_decay, length)
    decays = lax.all_gather(decay_tot[None, :], "seq", axis=0, tiled=True)
    weights = chain_weights(decays, parents, count)
    select = (blocks == mine).astype(jnp.float32)
    own_row = jnp.einsum("b,bah->ah", select, weights, precision=highest)
    own_col = jnp.einsum("a,bah->bh", select, weights, precision=highest)
    coef = own_row
    s_in = jnp.einsum(
        "kh,khnp->hnp",
        coef,
        lax.all_gather(loc_end[None], "seq", axis=0, tiled=True).astype(jnp.float32),
        precision=highest,
    )
    coef = own_col
    g_out = jnp.einsum(
        "kh,khnp->hnp",
        coef,
        lax.all_gather(loc_adj[None], "seq", axis=0, tiled=True).astype(jnp.float32),
        precision=highest,
    )
    x_grad, b_part, c_part, decay_grad = block_grads(b_in, c_in, saved, decay_tot, s_in, g_out)
    b_grad, c_grad = lax.psum((b_part, c_part), "mp")
    return (x_grad, b_grad, c_grad, decay_grad)


def solution(mesh):
    return jax.shard_map(
        on_device,
        mesh=mesh,
        in_specs=(
            P("seq", "mp"),
            P("seq", "mp"),
            P("seq", None),
            P("seq", None),
            P("mp", "seq"),
            P(),
            P(),
        ),
        out_specs=(P("seq", "mp"), P("seq", None), P("seq", None), P("mp", "seq")),
        check_vma=False,
    )
```

profile of v0, /device:TPU:1, one launch (start us, length us, event | category | flops | bytes accessed | tf_op | source)
XLA Modules:
  0.0 679.3 jit_solution(6052182643826448586)
XLA Ops:
  11.8 4.6 broadcast_multiply_fusion
  23.9 4.1 fusion.82
  29.6 65.1 %all-reduce = f32[512]{0:T(512)S(1)} all-reduce(f32[512]{0:T(512)S(1)} %dynamic-update-slice), channel_id=2, replica_groups=mesh['seq'=32,'mp'=8] {'seq'}, use_global_device_ids=true, to_apply=%add | all-reduce | flops 512 | bytes 4096
  94.8 23.7 %while.33 = (s32[]{:T(128)}, f32[32,32,16]{1,2,0:T(8,128)S(1)}, f32[32,16]{0,1:T(8,128)S(1)}, s32[32]{0:T(128)S(1)}, f32[32,16]{0,1:T(8,128)S(1)}, /*index=5*/s32[32]{0:T(128)S(1)}, s32[]{:T(128)}, s32[]{:T(128)}) while((s32[]{:T(128)}, f32[32,32,16]{1,2,0:T(8,128)S(1)}, f32[32,16]{0,1:T(8,128)S(1)}, s32[32]{0:T(128)S(1)}, ...), condition=%wide.region_5.6_spmd.clone, body=%wide.region_3.5_spmd.clone.sunk | while | flops 252963 | bytes 156768 | solution.py:28
  123.2 5.9 multiply_reduce_fusion.1
  129.1 92.9 %all-gather.6.cloned.1.call-done = bf16[512,128,64]{1,2,0:T(8,128)(2,1)} async-done(((bf16[16,128,64]{1,2,0:T(8,128)(2,1)}), bf16[512,128,64]{1,2,0:T(8,128)(2,1)}) %all-gather.6.cloned.1.call-update) | async-done | bytes 8388624 | tf_op jit(solution)/shard_map/all_gather | solution.py:128
  222.0 5.9 multiply_reduce_fusion.2
  228.0 379.1 %while.34 = (s32[]{:T(128)}, f32[512,128]{1,0:T(8,128)S(1)}, f32[512,128]{1,0:T(8,128)S(1)}, f32[16,512,64]{1,2,0:T(8,128)}, f32[16,512]{1,0:T(8,128)}, /*index=...) while((s32[]{:T(128)}, f32[512,128]{1,0:T(8,128)S(1)}, ...), condition=%wide.region_15.16_spmd.clone.clone, body=%wide.region_6.0_spmd.clone.clone.sunk | while | flops 1416156160 | bytes 14705120 | solution.py:101
  233.8 3.5 fusion.150
  257.5 3.5 fusion.150
  281.2 3.5 fusion.150
  304.9 3.5 fusion.150
  328.6 3.5 fusion.150
  352.3 3.5 fusion.150
  376.0 3.5 fusion.150
  399.7 3.5 fusion.150
  423.4 3.5 fusion.150
  447.1 3.5 fusion.150
  470.8 3.5 fusion.150
  494.5 3.5 fusion.150
  541.9 3.5 fusion.150
  565.6 3.5 fusion.150
  589.2 3.5 fusion.150
  610.8 58.6 %all-reduce.4.cloned.1.call-done = (f32[512,128]{1,0:T(8,128)}, f32[512,128]{1,0:T(8,128)}) async-done(((f32[512,128]{1,0:T(8,128)}, f32[512,128]{1,0:T(8,128)}), (f32[512,128]{1,0:T(8,128)}, f32[512,128]{1,0:T(8,128)})) %all-reduce.4.cloned.1.call-update) | async-done | bytes 524304 | tf_op jit(solution)/shard_map/psum | solution.py:132
  (789 shorter events, 341.4 us)
Async XLA Ops:
  7.2 116.1 %all-gather.8.cloned.1.call-start = ((), (), s32[]{:S(2)}) async-start(), calls=%async_computation.1 | async-start | bytes 8650752 | tf_op jit(solution)/shard_map/all_gather | solution.py:121
  20.9 201.1 %all-gather.6.cloned.1.call-start = ((), (), s32[]{:S(2)}) async-start(), calls=%async_computation | async-start | bytes 8650752 | tf_op jit(solution)/shard_map/all_gather | solution.py:128
  23.9 4.2 copy-start.7
  23.9 71.0 %copy-start.6 = (s32[32]{0:T(128)S(1)}, s32[32]{0:T(128)}, u32[]{:S(2)}) copy-start(s32[32]{0:T(128)} %param.16) | copy-start | bytes 388
  28.0 641.4 %all-reduce.4.cloned.1.call-start = ((), (), s32[]{:S(2)}) async-start(), calls=%async_computation.2 | async-start | bytes 1048576 | tf_op jit(solution)/shard_map/psum | solution.py:132
  247.0 4.6 copy-start.5
  265.1 3.6 copy-start.8
  270.7 4.6 copy-start.5
  288.8 3.6 copy-start.8
  294.4 4.6 copy-start.5
  318.1 4.6 copy-start.5
  341.8 4.6 copy-start.5
  365.5 4.6 copy-start.5
  389.2 4.6 copy-start.5
  407.3 3.6 copy-start.8
  412.9 4.6 copy-start.5
  436.6 4.6 copy-start.5
  460.3 4.6 copy-start.5
  484.0 4.6 copy-start.5
  507.7 4.6 copy-start.5
  531.4 4.6 copy-start.5
  555.1 4.6 copy-start.5
  578.7 4.6 copy-start.5
  602.4 4.6 copy-start.5
  (33 other events, 84.1 us)
Sparse Core Ops, SparseCore 0:
  21.0 102.1 all-gather.7
  126.4 95.6 all-gather.5
  608.0 61.3 all-reduce.3
where the time goes:
time: 686 us; the launch traced here: 679 us
  matrix products  248 us (36%)
  waiting for transfers between devices  152 us (22%)
  other arithmetic  85.3 us (12%)
  local copies, waits for them, and re-layouts  79.6 us (12%)
  blocking collectives  65.1 us (9%)
  loops' own time  34.3 us (5%)
  between operations  14.5 us (2%)
    all_gather x1, waiting for transfers between devices, on_device(): lax.all_gather(loc_adj[None], 'seq', axis=0, tiled=True).astype(jnp.float32)  92.9 us
    unnamed x1, blocking collectives  65.1 us
    psum x1, waiting for transfers between devices, on_device(): b_grad, c_grad = lax.psum((b_part, c_part), 'mp')  58.6 us
    dot_general x16, matrix products, one_head(): pairs = jnp.dot(dk, xk.T, precision=highest)  55.4 us
    dot_general x16, matrix products, one_head(): jnp.dot(dsc.T, dk, precision=highest) + ee[:, None] * bgo  45.1 us
    dot_general x16, matrix products, one_head(): jnp.dot(dpr, bmat, precision=highest)  36.9 us
    dynamic_slice x96, local copies, waits for them, and re-layouts, block_grads(): lax.scan(one_head, (zero_n, zero_n), items)  35.4 us
    another operation x1, loops' own time, block_grads(): lax.scan(one_head, (zero_n, zero_n), items)  32.9 us
  transfers between devices with their start and end apart: 3, of which 3 were waited for; matrix products, arithmetic and copies ran while one was open for 6% of the time, Pallas kernels for 0%

commit v1 on v0

v1 whole, which is shorter than its diff:
```python
import functools
import math

import jax
import jax.numpy as jnp
from jax import lax
from jax.experimental import pallas as pl
from jax.experimental.pallas import tpu as pltpu
from jax.sharding import PartitionSpec as P

f32 = jnp.float32
bf16 = jnp.bfloat16
MESH = pl.DeviceIdType.MESH
LOG2E = math.log2(math.e)

ROWS = 512
NST = 128
NH = 16
WID = 64
CH = NH * WID
TILE = 128
NT = ROWS // TILE
NY = 4
NZ = 8
NB = NY * NZ
QW = CH // NY
RW = NST // NZ
NMP = 8
SHARE = ROWS // NMP
CUT1, CUT2 = 3, 6
STEPS = 4
DZ_ORDER = (4, 3, 5, 2, 6, 1, 7, 0)


def dot(a, b):
    return jnp.dot(a, b, preferred_element_type=f32)


def dot_t(a, b):
    return lax.dot_general(a, b, (((1,), (1,)), ((), ())), preferred_element_type=f32)


def dot_0(a, b):
    return lax.dot_general(a, b, (((0,), (0,)), ((), ())), preferred_element_type=f32)


def split3(v):
    hi = v.astype(bf16)
    rest = v - hi.astype(f32)
    mid = rest.astype(bf16)
    low = (rest - mid.astype(f32)).astype(bf16)
    return hi, mid, low


def running(v, tri, reverse):
    tall = jnp.concatenate([v[:, TILE * i : TILE * (i + 1)] for i in range(NT)], axis=0)
    hi, mid, low = split3(tall)
    part = dot(hi, tri) + dot(mid, tri) + dot(low, tri)
    whole = jnp.sum(tall, axis=1, keepdims=True)
    pieces = [None] * NT
    carry = jnp.zeros((NH, 1), f32)
    order = range(NT - 1, -1, -1) if reverse else range(NT)
    for i in order:
        rows = slice(NH * i, NH * (i + 1))
        pieces[i] = part[rows] + carry
        carry = carry + whole[rows]
    return jnp.concatenate(pieces, axis=1)


def halves_of(v):
    hi = v.astype(bf16)
    return hi, (v - hi.astype(f32)).astype(bf16)


def kernel(
    lengths,
    prow,
    x_hbm,
    dy_hbm,
    b_ref,
    c_ref,
    logd_ref,
    xg_hbm,
    db_out,
    dc_out,
    dl_ref,
    x_v,
    dy_v,
    dx_v,
    eex_v,
    esdy_v,
    eexp_v,
    bt_v,
    ct_v,
    ccol_v,
    crow_v,
    last_v,
    st_v,
    mt_v,
    rowq_v,
    colq_v,
    tab_v,
    tab_s,
    send1,
    recv1,
    decx,
    decr,
    f_v,
    r_v,
    send2,
    recv2,
    part_v,
    rbuf,
    load_sem,
    out_sem,
    tab_sem,
    send_sem,
    recv_sem,
    own_sem,
):
    me = lax.axis_index("seq")
    mp = lax.axis_index("mp")
    my_y = lax.rem(me, NY)
    my_z = me // NY

    def group(i):
        return lax.rem(my_y + i, NY)

    def peer(i, dz):
        return lax.rem(my_z + dz, NZ) * NY + group(i)

    def lanes(q):
        return pl.ds(pl.multiple_of(q * QW, QW), QW)

    def to_seq(src, dst, j, k):
        pltpu.make_async_remote_copy(
            src_ref=src,
            dst_ref=dst,
            send_sem=send_sem.at[k],
            recv_sem=recv_sem.at[k],
            device_id={"seq": j},
            device_id_type=MESH,
        ).start()

    def to_mp(src, dst, j, k):
        pltpu.make_async_remote_copy(
            src_ref=src,
            dst_ref=dst,
            send_sem=send_sem.at[k],
            recv_sem=recv_sem.at[k],
            device_id={"mp": j},
            device_id_type=MESH,
        ).start()

    def settle(like, sem):
        pltpu.make_async_copy(like, like, sem).wait()

    loads = []
    for ref, buf, base in ((x_hbm, x_v, 0), (dy_hbm, dy_v, NY)):
        for i in range(NY):
            q = group(i)
            load = pltpu.make_async_copy(ref.at[:, lanes(q)], buf.at[:, lanes(q)], load_sem.at[base + i])
            load.start()
            loads.append(load)

    barrier = pltpu.get_barrier_semaphore()
    for i in range(NY):
        for dz in DZ_ORDER:
            if i or dz:
                pl.semaphore_signal(barrier, inc=1, device_id={"seq": peer(i, dz)}, device_id_type=MESH)
    for k in range(1, NMP):
        pl.semaphore_signal(barrier, inc=1, device_id={"mp": lax.rem(mp + k, NMP)}, device_id_type=MESH)

    length = lengths[me]

    ti = lax.broadcasted_iota(jnp.int32, (TILE, TILE), 0)
    tj = lax.broadcasted_iota(jnp.int32, (TILE, TILE), 1)
    upto = jnp.where(ti <= tj, 1.0, 0.0).astype(bf16)
    lane = lax.broadcasted_iota(jnp.int32, (NH, ROWS), 1)
    live = lane < length
    logd = jnp.where(live, logd_ref[...] * LOG2E, 0.0)
    cum = running(logd, upto, False)
    last = cum[:, ROWS - 1 : ROWS]
    last_v[...] = jnp.broadcast_to(last, (NH, TILE))
    ee = jnp.where(live, jnp.exp2(last - cum), 0.0)
    es = jnp.exp2(cum)
    ee_hi = ee.astype(bf16).astype(f32)
    es_hi = es.astype(bf16).astype(f32)
    stack = jnp.concatenate(
        [ee_hi, ee - ee_hi, es_hi, es - es_hi, cum, jnp.zeros((NST - 5 * NH, ROWS), f32)], axis=0
    )
    cols = stack.T
    cols_b = cols.astype(bf16)
    bt_hi, bt_lo = halves_of(b_ref[...].T)
    bt_v[0] = bt_hi
    bt_v[1] = bt_lo

    er = lax.broadcasted_iota(jnp.int32, (NST, QW), 0)
    eh = lax.broadcasted_iota(jnp.int32, (NST, QW), 1) // WID

    def spread(q, base, rows=cols_b):
        head = eh + (q * (NH // NY) + base)
        return dot(rows, jnp.where((er == head) | (er == head + NH), 1.0, 0.0).astype(bf16))

    def state_of(t_v, wide):
        hi, low = halves_of(wide)
        total = dot(t_v[0], hi) + dot(t_v[1], hi) + dot(t_v[0], low)
        return hi, total.astype(bf16)

    for i in range(NY):
        q = group(i)
        e_wide = spread(q, 0)
        eexp_v[:, lanes(q)] = e_wide
        loads[i].wait()
        hi, loc = state_of(bt_v, x_v[:, lanes(q)] * e_wide)
        eex_v[:, lanes(q)] = hi
        decx[q] = spread(q, 2 * NH, cols_b[ROWS - RW :, :])[RW - 1 :, :]
        for r in range(NZ):
            send1[0, r * NY + q] = loc[RW * r : RW * (r + 1), :]
        if i == 0:
            pl.semaphore_wait(barrier, NB - 1 + NMP - 1)
        for dz in DZ_ORDER:
            if i or dz:
                j = peer(i, dz)
                to_seq(send1.at[0, j], recv1.at[0, me], j, 0)
        for dz in DZ_ORDER:
            if i or dz:
                j = peer(i, dz)
                to_seq(decx.at[q], decr.at[me], j, 2)

    ct_hi, ct_lo = halves_of(c_ref[...].T)
    ct_v[0] = ct_hi
    ct_v[1] = ct_lo
    row_live = lax.broadcasted_iota(jnp.int32, (ROWS, QW), 0) < length
    for i in range(NY):
        q = group(i)
        s_wide = spread(q, 2 * NH)
        loads[NY + i].wait()
        dy = jnp.where(row_live, dy_v[:, lanes(q)], 0.0)
        dy_v[:, lanes(q)] = dy
        hi, loc = state_of(ct_v, dy * s_wide)
        esdy_v[:, lanes(q)] = hi
        for r in range(NZ):
            send1[1, r * NY + q] = loc[RW * r : RW * (r + 1), :]
        for dz in DZ_ORDER:
            if i or dz:
                j = peer(i, dz)
                to_seq(send1.at[1, j], recv1.at[1, me], j, 1)
    own = [
        pltpu.make_async_copy(send1.at[0, me], recv1.at[0, me], own_sem.at[0]),
        pltpu.make_async_copy(send1.at[1, me], recv1.at[1, me], own_sem.at[1]),
        pltpu.make_async_copy(decx.at[my_y], decr.at[me], own_sem.at[2]),
    ]
    for copy in own:
        copy.start()

    bi = lax.broadcasted_iota(jnp.int32, (NB, NB), 0)
    bj = lax.broadcasted_iota(jnp.int32, (NB, NB), 1)
    par = jnp.broadcast_to(prow[...], (NB, NB))
    par_col = jnp.sum(jnp.where(bi == bj, par, 0), axis=1, keepdims=True)
    first = jnp.min(jnp.where(par == bi, bj, NB), axis=1, keepdims=True)
    sibling = jnp.min(jnp.where((par == par_col) & (bj > bi), bj, NB), axis=1, keepdims=True)
    tl = lax.broadcasted_iota(jnp.int32, (NB, TILE), 1)
    tab_v[...] = jnp.where(
        tl == 0, first, jnp.where(tl == 1, sibling, jnp.where(par_col < 0, NB, par_col))
    )
    tab = pltpu.make_async_copy(tab_v, tab_s, tab_sem)
    tab.start()

    st_v[...] = lax.dot_general(
        b_ref[...],
        c_ref[...],
        (((1,), (1,)), ((), ())),
        preferred_element_type=f32,
        precision=lax.Precision.HIGHEST,
    )
    mt_v[...] = jnp.zeros_like(mt_v)
    colq_v[...] = jnp.zeros_like(colq_v)
    for h in range(NH):
        crow_v[h] = cum[h : h + 1, :]
        ccol_v[h] = jnp.broadcast_to(cols[:, 4 * NH + h : 4 * NH + h + 1], (ROWS, TILE))
    left = lax.broadcasted_iota(jnp.int32, (ROWS, TILE), 1) < WID
    nil = jnp.zeros((ROWS, TILE), bf16)

    def pair(k, carry):
        span = pl.ds(pl.multiple_of(k * TILE, TILE), TILE)
        xk = x_v[:, span]
        dk = dy_v[:, span]
        xr = pltpu.roll(xk, WID, 1)
        dr = pltpu.roll(dk, WID, 1)
        xs, ds = [], []
        for s in range(2):
            hi, low = halves_of(jnp.where(left, xk, xr) if s == 0 else jnp.where(left, xr, xk))
            both = jnp.where(left, hi, low)
            xs.append(jnp.concatenate([both, both], axis=1))
            ds.append(halves_of(jnp.where(left, dk, dr) if s == 0 else jnp.where(left, dr, dk)))
        dg = [jnp.concatenate(d, axis=1) for d in ds]
        dn = [jnp.where(left, ds[0][0], nil), jnp.where(left, nil, ds[1][0])]
        dx = [jnp.zeros((TILE, TILE), f32) for _ in range(NT)]
        rowq = [[None] * NT, [None] * NT]
        colq = [[None] * NT, [None] * NT]
        for ib in range(NT):
            ts = slice(TILE * ib, TILE * (ib + 1))
            dt = jnp.concatenate([dn[0][ts, :], dn[1][ts, :]], axis=0)
            for jb in range(ib + 1):
                us = slice(TILE * jb, TILE * (jb + 1))
                score = st_v[us, ts]
                total = mt_v[us, ts]
                wide = []
                for s in range(2):
                    h = 2 * k + s
                    g = dot_t(xs[s][us, :], dg[s][ts, :])
                    diff = crow_v[h, :, ts] - ccol_v[h, us, :]
                    if ib == jb:
                        diff = jnp.where(tj >= ti, diff, -1e30)
                    e = jnp.exp2(diff)
                    dsc = e * score
                    total = total + e * g
                    wide.append(dsc.astype(bf16))
                    joint = dsc * g
                    down = jnp.sum(joint, axis=0, keepdims=True)
                    rowq[s][ib] = down if jb == 0 else rowq[s][ib] + down
                    colq[s][jb] = joint if ib == jb else colq[s][jb] + joint
                mt_v[us, ts] = total
                dx[jb] = dx[jb] + dot(jnp.concatenate(wide, axis=1), dt)
        for s in range(2):
            rowq_v[2 * k + s] = jnp.concatenate(rowq[s], axis=1)
        for jb in range(NT):
            us = slice(TILE * jb, TILE * (jb + 1))
            both = colq_v[us, :]
            for s in range(2):
                tot = jnp.sum(colq[s][jb], axis=1, keepdims=True)
                both = jnp.where(tj == 2 * NH + 2 * k + s, tot, both)
            colq_v[us, :] = both
            dx_v[us, span] = dx[jb]
        return carry

    lax.fori_loop(0, CUT1, pair, 0)

    tab.wait()
    for copy in own:
        copy.wait()
    f_v[NB] = jnp.zeros((RW, QW), f32)
    r_v[NB] = jnp.zeros((RW, QW), f32)
    settle(recv1.at[0, pl.ds(0, NB - 1)], recv_sem.at[0])
    settle(decr.at[pl.ds(0, NB - 1)], recv_sem.at[2])

    def forward(b, carry):
        state = f_v[tab_s[b, 2]]
        send2[0, b] = state.astype(bf16)
        f_v[b] = recv1[0, b].astype(f32) + decr[b] * state
        return carry

    def backward(k, carry):
        a = NB - 1 - k
        adj = r_v[tab_s[a, 0]]
        send2[1, a] = adj.astype(bf16)
        r_v[a] = recv1[1, a].astype(f32) + decr[a] * adj + r_v[tab_s[a, 1]]
        return carry

    def hand_back(w, k):
        for dz in DZ_ORDER:
            for i in range(NY):
                if i or dz:
                    j = peer(i, dz)
                    to_seq(send2.at[w, j], recv2.at[w, me], j, k)
        copy = pltpu.make_async_copy(send2.at[w, me], recv2.at[w, me], own_sem.at[3 + w])
        copy.start()
        return copy

    lax.fori_loop(0, NB, forward, 0)
    own_s = hand_back(0, 3)

    lax.fori_loop(CUT1, CUT2, pair, 0)

    settle(recv1.at[1, pl.ds(0, NB - 1)], recv_sem.at[1])
    lax.fori_loop(0, NB, backward, 0)
    own_g = hand_back(1, 4)

    lax.fori_loop(CUT2, NH // 2, pair, 0)

    b_hi, b_lo = halves_of(b_ref[...])
    c_hi, c_lo = halves_of(c_ref[...])
    mt_hi, mt_lo = halves_of(mt_v[...])
    db = dot(mt_hi, c_hi) + dot(mt_lo, c_hi) + dot(mt_hi, c_lo)
    dc = dot_0(mt_hi, b_hi) + dot_0(mt_lo, b_hi) + dot_0(mt_hi, b_lo)
    b_two = jnp.concatenate([b_hi, b_lo], axis=1)
    c_two = jnp.concatenate([c_hi, c_lo], axis=1)

    def arrived(w, q):
        return jnp.concatenate([recv2[w, r * NY + q] for r in range(NZ)], axis=0)

    def scatter(w, terms, k):
        part_v[w] = terms.astype(bf16)
        for d in (4, 3, 5, 2, 6, 1, 7):
            to = lax.rem(mp + d, NMP)
            to_mp(part_v.at[w, share_of(to)], rbuf.at[w, mp], to, k)
        copy = pltpu.make_async_copy(part_v.at[w, share_of(mp)], rbuf.at[w, mp], own_sem.at[5 + w])
        copy.start()
        return copy

    def share_of(k):
        return pl.ds(pl.multiple_of(k * SHARE, SHARE), SHARE)

    def spread_share(w, out, own_part, k):
        own_part.wait()
        settle(rbuf.at[w, pl.ds(0, NMP - 1)], recv_sem.at[k])
        share = rbuf[w, 0].astype(f32)
        for d in range(1, NMP):
            share = share + rbuf[w, d].astype(f32)
        out[share_of(mp), :] = share.astype(bf16)
        for d in (4, 3, 5, 2, 6, 1, 7):
            to_mp(out.at[share_of(mp), :], out.at[share_of(mp), :], lax.rem(mp + d, NMP), k + 1)

    own_s.wait()
    settle(recv2.at[0, pl.ds(0, NB - 1)], recv_sem.at[3])
    s_in = [arrived(0, q) for q in range(NY)]
    for q in range(NY):
        dc = dc + dot_t(esdy_v[:, QW * q : QW * (q + 1)], s_in[q])
    own_dc = scatter(0, dc, 5)
    acc = colq_v[...]
    sel_r = lax.broadcasted_iota(jnp.int32, (QW, TILE), 0) // WID
    sel_l = lax.broadcasted_iota(jnp.int32, (QW, TILE), 1)

    def picks(q, base):
        return jnp.where(sel_l == sel_r + (q * (NH // NY) + base), 1.0, 0.0).astype(bf16)

    for q in range(NY):
        chi = dot(c_two, jnp.concatenate([s_in[q], s_in[q]], axis=0))
        head = chi * esdy_v[:, QW * q : QW * (q + 1)].astype(f32)
        acc = acc + dot(head.astype(bf16), picks(q, 0))
    spread_share(0, dc_out, own_dc, 5)

    own_g.wait()
    settle(recv2.at[1, pl.ds(0, NB - 1)], recv_sem.at[4])
    g_out = [arrived(1, q) for q in range(NY)]
    for q in range(NY):
        db = db + dot_t(eex_v[:, QW * q : QW * (q + 1)], g_out[q])
    own_db = scatter(1, db, 7)

    gs = jnp.zeros((8, NST), f32)
    stores = []
    for q in range(NY):
        span = slice(QW * q, QW * (q + 1))
        bgo = dot(b_two, jnp.concatenate([g_out[q], g_out[q]], axis=0))
        dx_b = (dx_v[:, span] + eexp_v[:, span] * bgo).astype(bf16)
        eex = eex_v[:, span].astype(f32)
        esdy_v[:, span] = dx_b
        out = pltpu.make_async_copy(esdy_v.at[:, span], xg_hbm.at[:, span], out_sem.at[q])
        out.start()
        stores.append(out)
        acc = acc + dot((bgo * eex).astype(bf16), picks(q, NH))
        both = jnp.sum(g_out[q].astype(f32) * s_in[q].astype(f32), axis=0, keepdims=True)
        both_hi, both_lo = halves_of(jnp.broadcast_to(both, (8, QW)))
        gs = gs + dot(both_hi, picks(q, 0)) + dot(both_lo, picks(q, 0))
    flat = acc.T
    gs_col = gs.T[0:NH, 0:1]
    head = flat[0:NH]
    tail = flat[NH : 2 * NH]
    colq = flat[2 * NH : 3 * NH]
    since = jnp.where(ti >= tj, 1.0, 0.0).astype(bf16)
    before = jnp.where(ti < tj, 1.0, 0.0).astype(bf16)
    dec = jnp.exp2(last_v[:, 0:1])
    rowq = jnp.concatenate([rowq_v[h] for h in range(NH)], axis=0)
    total = running(rowq - colq + head, since, True) + running(tail, before, False) + dec * gs_col
    dl_ref[...] = jnp.where(live, total, 0.0)

    spread_share(1, db_out, own_db, 7)

    settle(send1.at[0, pl.ds(0, NB - 1)], send_sem.at[0])
    settle(send1.at[1, pl.ds(0, NB - 1)], send_sem.at[1])
    settle(decr.at[pl.ds(0, NB - 1)], send_sem.at[2])
    settle(send2.at[0, pl.ds(0, NB - 1)], send_sem.at[3])
    settle(send2.at[1, pl.ds(0, NB - 1)], send_sem.at[4])
    for w in range(2):
        settle(rbuf.at[w, pl.ds(0, NMP - 1)], send_sem.at[5 + 2 * w])
        settle(rbuf.at[w, pl.ds(0, NMP - 1)], send_sem.at[6 + 2 * w])
    for out in stores:
        out.wait()
    settle(rbuf.at[0, pl.ds(0, NMP - 1)], recv_sem.at[6])
    settle(rbuf.at[1, pl.ds(0, NMP - 1)], recv_sem.at[8])


def finish(xg_ref, db_ref, dc_ref, dl_ref, xg_out, db_out, dc_out, dl_out):
    xg_out[...] = xg_ref[...].astype(f32)

    @pl.when(pl.program_id(0) == 0)
    def _():
        db_out[...] = db_ref[...].astype(f32)
        dc_out[...] = dc_ref[...].astype(f32)
        dl_out[...] = dl_ref[...]


def on_device(x_in, dy_out, b_in, c_in, log_decay, parents, lengths):
    vmem = pl.BlockSpec(memory_space=pltpu.VMEM)
    smem = pl.BlockSpec(memory_space=pltpu.SMEM)
    anywhere = pl.BlockSpec(memory_space=pl.ANY)
    wide = (ROWS, CH)
    dma = pltpu.SemaphoreType.DMA
    given = pl.pallas_call(
        kernel,
        out_shape=(
            jax.ShapeDtypeStruct(wide, bf16),
            jax.ShapeDtypeStruct((ROWS, NST), bf16),
            jax.ShapeDtypeStruct((ROWS, NST), bf16),
            jax.ShapeDtypeStruct((NH, ROWS), f32),
        ),
        in_specs=[smem, vmem, anywhere, anywhere, vmem, vmem, vmem],
        out_specs=(anywhere, vmem, vmem, vmem),
        scratch_shapes=[
            pltpu.VMEM(wide, f32),
            pltpu.VMEM(wide, f32),
            pltpu.VMEM(wide, f32),
            pltpu.VMEM(wide, bf16),
            pltpu.VMEM(wide, bf16),
            pltpu.VMEM(wide, f32),
            pltpu.VMEM((2, NST, ROWS), bf16),
            pltpu.VMEM((2, NST, ROWS), bf16),
            pltpu.VMEM((NH, ROWS, TILE), f32),
            pltpu.VMEM((NH, 1, ROWS), f32),
            pltpu.VMEM((NH, TILE), f32),
            pltpu.VMEM((ROWS, ROWS), f32),
            pltpu.VMEM((ROWS, ROWS), f32),
            pltpu.VMEM((NH, 1, ROWS), f32),
            pltpu.VMEM((ROWS, TILE), f32),
            pltpu.VMEM((NB, TILE), jnp.int32),
            pltpu.SMEM((NB, TILE), jnp.int32),
            pltpu.VMEM((2, NB, RW, QW), bf16),
            pltpu.VMEM((2, NB, RW, QW), bf16),
            pltpu.VMEM((NY, 1, QW), f32),
            pltpu.VMEM((NB, 1, QW), f32),
            pltpu.VMEM((NB + 1, RW, QW), f32),
            pltpu.VMEM((NB + 1, RW, QW), f32),
            pltpu.VMEM((2, NB, RW, QW), bf16),
            pltpu.VMEM((2, NB, RW, QW), bf16),
            pltpu.VMEM((2, ROWS, NST), bf16),
            pltpu.VMEM((2, NMP, SHARE, NST), bf16),
            dma((2 * NY,)),
            dma((NY,)),
            dma,
            dma((9,)),
            dma((9,)),
            dma((7,)),
        ],
        compiler_params=pltpu.CompilerParams(
            collective_id=0, has_side_effects=True, vmem_limit_bytes=56 * 1024 * 1024
        ),
    )(lengths, parents.reshape(1, NB), x_in, dy_out, b_in, c_in, log_decay)
    step = ROWS // STEPS
    rows = pl.BlockSpec((step, CH), lambda i: (i, 0))
    whole = pl.BlockSpec((ROWS, NST), lambda i: (0, 0))
    decays = pl.BlockSpec((NH, ROWS), lambda i: (0, 0))
    return tuple(
        pl.pallas_call(
            finish,
            grid=(STEPS,),
            out_shape=(
                jax.ShapeDtypeStruct(wide, f32),
                jax.ShapeDtypeStruct((ROWS, NST), f32),
                jax.ShapeDtypeStruct((ROWS, NST), f32),
                jax.ShapeDtypeStruct((NH, ROWS), f32),
            ),
            in_specs=[rows, whole, whole, decays],
            out_specs=(rows, whole, whole, decays),
        )(*given)
    )


def solution(mesh):
    return jax.shard_map(
        on_device,
        mesh=mesh,
        in_specs=(
            P("seq", "mp"),
            P("seq", "mp"),
            P("seq", None),
            P("seq", None),
            P("mp", "seq"),
            P(),
            P(),
        ),
        out_specs=(P("seq", "mp"), P("seq", None), P("seq", None), P("mp", "seq")),
        check_vma=False,
    )
```

time: 686 us -> 53.4 us (0.08)
  matrix products: 248 us -> 0 us
  waiting for transfers between devices: 152 us -> 0 us
  other arithmetic: 85.3 us -> 0 us
  local copies, waits for them, and re-layouts: 79.6 us -> 0 us
  blocking collectives: 65.1 us -> 0 us
  Pallas kernels: 0 us -> 52.6 us
  loops' own time: 34.3 us -> 0 us
  between operations: 14.5 us -> 0.64 us
    dot_general x165 -> x0, matrix products: 248 us -> none  [the longest x16 55.4 us: one_head(): pairs = jnp.dot(dk, xk.T, precision=highest)]
    all_gather x2 -> x0, waiting for transfers between devices: 93.7 us -> none  [the longest x1 92.9 us: on_device(): lax.all_gather(loc_adj[None], 'seq', axis=0, tiled=True).astype(jnp.float32)]
    unnamed x1 -> x0, blocking collectives: 65.1 us -> none
    psum x1 -> x0, waiting for transfers between devices: 58.6 us -> none  [on_device(): b_grad, c_grad = lax.psum((b_part, c_part), 'mp')]
    pallas_call x0 -> x2, Pallas kernels: none -> 52.6 us  [the longest x1 48.7 us: on_device(): pl.pallas_call(kernel, out_shape=(jax.ShapeDtypeStruct(wide, bf16), jax.S...]
    dynamic_slice x96 -> x0, local copies, waits for them, and re-layouts: 35.4 us -> none  [block_grads(): lax.scan(one_head, (zero_n, zero_n), items)]
    another operation x2 -> x0, loops' own time: 34.3 us -> none  [the longest x1 32.9 us: block_grads(): lax.scan(one_head, (zero_n, zero_n), items)]
    reduce_sum x65 -> x0, other arithmetic: 27.9 us -> none  [the longest x32 20.4 us: one_head(): extra = jnp.sum(tail) + dk_dec * jnp.sum(gk * hk)]
  transfers between devices with their start and end apart: 3 -> 0, of which waited for: 3 -> 0; matrix products, arithmetic and copies ran while one was open for 6% -> 0% of each run, Pallas kernels for 0% -> 0%
where the time goes in v1:
time: 53.4 us; the launch traced here: 53.2 us
  Pallas kernels  52.6 us (99%)
  between operations  0.64 us (1%)
    pallas_call x1, Pallas kernels, on_device(): pl.pallas_call(kernel, out_shape=(jax.ShapeDtypeStruct(wide, bf16), jax.S...  48.7 us
    pallas_call x1, Pallas kernels, on_device(): pl.pallas_call(finish, grid=(STEPS,), out_shape=(jax.ShapeDtypeStruct(wid...  3.9 us

profile of v1, /device:TPU:1, one launch (start us, length us, event | category | flops | bytes accessed | tf_op | source)
XLA Modules:
  0.0 53.2 jit_solution(10154547124516928012)
XLA Ops:
  0.6 48.7 %shard_map.102 = (bf16[512,1024]{1,0:T(8,128)(2,1)}, bf16[512,128]{1,0:T(8,128)(2,1)}, bf16[512,128]{1,0:T(8,128)(2,1)}, f32[16,512]{1,0:T(8,128)}) custom-call(s32[32]{0:T(128)} %lengths.1, s32[1,32]{1,0:T(1,128)} %bitcast.1, f32[512,1024]{1,0:T(8,128)} %x_hbm.1, f32[512,1024]{1,0:T(8,128)} %dy_hbm.1, f32[512,128]{1,0:T(8,128)} %b_ref.1, f32[512,128]{1,0:T(8,128)} %c_ref.1, ...), custom_call_target="tpu_custom_call" | custom-call | tf_op jit(solution)/shard_map/pallas_call | solution.py:500
  49.3 3.9 %shard_map.103 = (f32[512,1024]{1,0:T(8,128)}, f32[512,128]{1,0:T(8,128)}, f32[512,128]{1,0:T(8,128)}, f32[16,512]{1,0:T(8,128)}) custom-call(bf16[512,1024]{1,0:T(8,128)(2,1)} %get-tuple-element.8.xg_ref, bf16[512,128]{1,0:T(8,128)(2,1)} %get-tuple-element.9.db_ref, bf16[512,128]{1,0:T(8,128)(2,1)} %get-tuple-element.10.dc_ref, ...), custom_call_target="tpu_custom_call" | custom-call | tf_op jit(solution)/shard_map/pallas_call | solution.py:554

commit v2 on v1

--- a/solution.py
+++ b/solution.py
@@ -28,7 +28,6 @@
 NMP = 8
 SHARE = ROWS // NMP
 CUT1, CUT2 = 3, 6
-STEPS = 4
 DZ_ORDER = (4, 3, 5, 2, 6, 1, 7, 0)
 
 
@@ -80,13 +79,12 @@
     b_ref,
     c_ref,
     logd_ref,
-    xg_hbm,
+    dx_v,
     db_out,
     dc_out,
     dl_ref,
     x_v,
     dy_v,
-    dx_v,
     eex_v,
     esdy_v,
     eexp_v,
@@ -112,7 +110,6 @@
     part_v,
     rbuf,
     load_sem,
-    out_sem,
     tab_sem,
     send_sem,
     recv_sem,
@@ -439,16 +436,11 @@
     own_db = scatter(1, db, 7)
 
     gs = jnp.zeros((8, NST), f32)
-    stores = []
     for q in range(NY):
         span = slice(QW * q, QW * (q + 1))
         bgo = dot(b_two, jnp.concatenate([g_out[q], g_out[q]], axis=0))
-        dx_b = (dx_v[:, span] + eexp_v[:, span] * bgo).astype(bf16)
+        dx_v[:, span] = dx_v[:, span] + eexp_v[:, span] * bgo
         eex = eex_v[:, span].astype(f32)
-        esdy_v[:, span] = dx_b
-        out = pltpu.make_async_copy(esdy_v.at[:, span], xg_hbm.at[:, span], out_sem.at[q])
-        out.start()
-        stores.append(out)
         acc = acc + dot((bgo * eex).astype(bf16), picks(q, NH))
         both = jnp.sum(g_out[q].astype(f32) * s_in[q].astype(f32), axis=0, keepdims=True)
         both_hi, both_lo = halves_of(jnp.broadcast_to(both, (8, QW)))
@@ -475,20 +467,21 @@
     for w in range(2):
         settle(rbuf.at[w, pl.ds(0, NMP - 1)], send_sem.at[5 + 2 * w])
         settle(rbuf.at[w, pl.ds(0, NMP - 1)], send_sem.at[6 + 2 * w])
-    for out in stores:
-        out.wait()
     settle(rbuf.at[0, pl.ds(0, NMP - 1)], recv_sem.at[6])
     settle(rbuf.at[1, pl.ds(0, NMP - 1)], recv_sem.at[8])
 
 
-def finish(xg_ref, db_ref, dc_ref, dl_ref, xg_out, db_out, dc_out, dl_out):
-    xg_out[...] = xg_ref[...].astype(f32)
-
-    @pl.when(pl.program_id(0) == 0)
-    def _():
-        db_out[...] = db_ref[...].astype(f32)
-        dc_out[...] = dc_ref[...].astype(f32)
-        dl_out[...] = dl_ref[...]
+def finish(xg_ref, db_ref, dc_ref, dl_ref, xg_out, db_out, dc_out, dl_out, db_v, dc_v, sem):
+    copies = [pltpu.make_async_copy(xg_ref, xg_out, sem.at[0]), pltpu.make_async_copy(dl_ref, dl_out, sem.at[1])]
+    for copy in copies:
+        copy.start()
+    for k, (low, wide, out) in enumerate(((db_ref, db_v, db_out), (dc_ref, dc_v, dc_out))):
+        wide[...] = low[...].astype(f32)
+        copy = pltpu.make_async_copy(wide, out, sem.at[2 + k])
+        copy.start()
+        copies.append(copy)
+    for copy in copies:
+        copy.wait()
 
 
 def on_device(x_in, dy_out, b_in, c_in, log_decay, parents, lengths):
@@ -500,15 +493,14 @@
     given = pl.pallas_call(
         kernel,
         out_shape=(
-            jax.ShapeDtypeStruct(wide, bf16),
-            jax.ShapeDtypeStruct((ROWS, NST), bf16),
-            jax.ShapeDtypeStruct((ROWS, NST), bf16),
-            jax.ShapeDtypeStruct((NH, ROWS), f32),
+            pltpu.VMEM(wide, f32),
+            pltpu.VMEM((ROWS, NST), bf16),
+            pltpu.VMEM((ROWS, NST), bf16),
+            pltpu.VMEM((NH, ROWS), f32),
         ),
         in_specs=[smem, vmem, anywhere, anywhere, vmem, vmem, vmem],
-        out_specs=(anywhere, vmem, vmem, vmem),
+        out_specs=(vmem, vmem, vmem, vmem),
         scratch_shapes=[
-            pltpu.VMEM(wide, f32),
             pltpu.VMEM(wide, f32),
             pltpu.VMEM(wide, f32),
             pltpu.VMEM(wide, bf16),
@@ -536,33 +528,32 @@
             pltpu.VMEM((2, ROWS, NST), bf16),
             pltpu.VMEM((2, NMP, SHARE, NST), bf16),
             dma((2 * NY,)),
-            dma((NY,)),
             dma,
             dma((9,)),
             dma((9,)),
             dma((7,)),
         ],
         compiler_params=pltpu.CompilerParams(
-            collective_id=0, has_side_effects=True, vmem_limit_bytes=56 * 1024 * 1024
+            collective_id=0, has_side_effects=True, vmem_limit_bytes=52 * 1024 * 1024
         ),
     )(lengths, parents.reshape(1, NB), x_in, dy_out, b_in, c_in, log_decay)
-    step = ROWS // STEPS
-    rows = pl.BlockSpec((step, CH), lambda i: (i, 0))
-    whole = pl.BlockSpec((ROWS, NST), lambda i: (0, 0))
-    decays = pl.BlockSpec((NH, ROWS), lambda i: (0, 0))
     return tuple(
         pl.pallas_call(
             finish,
-            grid=(STEPS,),
             out_shape=(
                 jax.ShapeDtypeStruct(wide, f32),
                 jax.ShapeDtypeStruct((ROWS, NST), f32),
                 jax.ShapeDtypeStruct((ROWS, NST), f32),
                 jax.ShapeDtypeStruct((NH, ROWS), f32),
             ),
-            in_specs=[rows, whole, whole, decays],
-            out_specs=(rows, whole, whole, decays),
-        )(*given)
+            in_specs=[vmem] * 4,
+            out_specs=(anywhere,) * 4,
+            scratch_shapes=[
+                pltpu.VMEM((ROWS, NST), f32),
+                pltpu.VMEM((ROWS, NST), f32),
+                dma((4,)),
+            ],
+        )(*(pltpu.with_memory_space_constraint(g, pltpu.VMEM) for g in given))
     )
 
 

time: 53.4 us -> 50.2 us (0.940)
  Pallas kernels: 52.6 us -> 49.5 us
    pallas_call x2, Pallas kernels: 52.6 us -> 49.5 us  [the longest x1 48 us: on_device(): pl.pallas_call(kernel, out_shape=(pltpu.VMEM(wide, f32), pltpu.VMEM((ROWS...]
where the time goes in v2:
time: 50.2 us; the launch traced here: 50.1 us
  Pallas kernels  49.5 us (99%)
  between operations  0.64 us (1%)
    pallas_call x1, Pallas kernels, on_device(): pl.pallas_call(kernel, out_shape=(pltpu.VMEM(wide, f32), pltpu.VMEM((ROWS...  48 us
    pallas_call x1, Pallas kernels, on_device(): pl.pallas_call(finish, out_shape=(jax.ShapeDtypeStruct(wide, f32), jax.Sh...  1.53 us

profile of v2, /device:TPU:1, one launch (start us, length us, event | category | flops | bytes accessed | tf_op | source)
XLA Modules:
  0.0 50.1 jit_solution(18107240818596644981)
XLA Ops:
  0.6 48.0 %shard_map.102 = (f32[512,1024]{1,0:T(8,128)S(1)}, bf16[512,128]{1,0:T(8,128)(2,1)S(1)}, bf16[512,128]{1,0:T(8,128)(2,1)S(1)}, f32[16,512]{1,0:T(8,128)S(1)}) custom-call(s32[32]{0:T(128)} %lengths.1, s32[1,32]{1,0:T(1,128)} %bitcast.1, f32[512,1024]{1,0:T(8,128)} %x_hbm.1, f32[512,1024]{1,0:T(8,128)} %dy_hbm.1, f32[512,128]{1,0:T(8,128)} %b_ref.1, ...), custom_call_target="tpu_custom_call" | custom-call | tf_op jit(solution)/shard_map/pallas_call | solution.py:493
  48.6 1.5 %shard_map.103 = (f32[512,1024]{1,0:T(8,128)}, f32[512,128]{1,0:T(8,128)}, f32[512,128]{1,0:T(8,128)}, f32[16,512]{1,0:T(8,128)}) custom-call(f32[512,1024]{1,0:T(8,128)S(1)} %get-tuple-element.8.xg_ref, bf16[512,128]{1,0:T(8,128)(2,1)S(1)} %get-tuple-element.9.db_ref, bf16[512,128]{1,0:T(8,128)(2,1)S(1)} %get-tuple-element.10.dc_ref, ...), custom_call_target="tpu_custom_call" | custom-call | tf_op jit(solution)/shard_map/pallas_call | solution.py:541

commit v3 on v2

--- a/solution.py
+++ b/solution.py
@@ -72,17 +72,22 @@
 
 
 def kernel(
-    lengths,
-    prow,
+    lengths_hbm,
+    prow_hbm,
     x_hbm,
     dy_hbm,
-    b_ref,
-    c_ref,
-    logd_ref,
+    b_hbm,
+    c_hbm,
+    logd_hbm,
     dx_v,
     db_out,
     dc_out,
     dl_ref,
+    lengths,
+    prow,
+    b_ref,
+    c_ref,
+    logd_ref,
     x_v,
     dy_v,
     eex_v,
@@ -103,6 +108,7 @@
     recv1,
     decx,
     decr,
+    decw,
     f_v,
     r_v,
     send2,
@@ -153,12 +159,17 @@
         pltpu.make_async_copy(like, like, sem).wait()
 
     loads = []
-    for ref, buf, base in ((x_hbm, x_v, 0), (dy_hbm, dy_v, NY)):
-        for i in range(NY):
-            q = group(i)
-            load = pltpu.make_async_copy(ref.at[:, lanes(q)], buf.at[:, lanes(q)], load_sem.at[base + i])
-            load.start()
-            loads.append(load)
+
+    def load(src, dst):
+        copy = pltpu.make_async_copy(src, dst, load_sem.at[len(loads)])
+        copy.start()
+        loads.append(copy)
+        return copy
+
+    logd_in = load(logd_hbm, logd_ref)
+    lengths_in = load(lengths_hbm, lengths)
+    b_in = load(b_hbm, b_ref)
+    x_in = [load(x_hbm.at[:, lanes(group(i))], x_v.at[:, lanes(group(i))]) for i in range(NY)]
 
     barrier = pltpu.get_barrier_semaphore()
     for i in range(NY):
@@ -168,7 +179,13 @@
     for k in range(1, NMP):
         pl.semaphore_signal(barrier, inc=1, device_id={"mp": lax.rem(mp + k, NMP)}, device_id_type=MESH)
 
-    length = lengths[me]
+    c_in = load(c_hbm, c_ref)
+    dy_in = [load(dy_hbm.at[:, lanes(group(i))], dy_v.at[:, lanes(group(i))]) for i in range(NY)]
+    prow_in = load(prow_hbm, prow)
+
+    lengths_in.wait()
+    length = lengths[0, me]
+    logd_in.wait()
 
     ti = lax.broadcasted_iota(jnp.int32, (TILE, TILE), 0)
     tj = lax.broadcasted_iota(jnp.int32, (TILE, TILE), 1)
@@ -187,7 +204,9 @@
         [ee_hi, ee - ee_hi, es_hi, es - es_hi, cum, jnp.zeros((NST - 5 * NH, ROWS), f32)], axis=0
     )
     cols = stack.T
+    decx[0] = cols[ROWS - 1 :, :]
     cols_b = cols.astype(bf16)
+    b_in.wait()
     bt_hi, bt_lo = halves_of(b_ref[...].T)
     bt_v[0] = bt_hi
     bt_v[1] = bt_lo
@@ -195,9 +214,9 @@
     er = lax.broadcasted_iota(jnp.int32, (NST, QW), 0)
     eh = lax.broadcasted_iota(jnp.int32, (NST, QW), 1) // WID
 
-    def spread(q, base, rows=cols_b):
+    def spread(q, base):
         head = eh + (q * (NH // NY) + base)
-        return dot(rows, jnp.where((er == head) | (er == head + NH), 1.0, 0.0).astype(bf16))
+        return dot(cols_b, jnp.where((er == head) | (er == head + NH), 1.0, 0.0).astype(bf16))
 
     def state_of(t_v, wide):
         hi, low = halves_of(wide)
@@ -208,10 +227,9 @@
         q = group(i)
         e_wide = spread(q, 0)
         eexp_v[:, lanes(q)] = e_wide
-        loads[i].wait()
+        x_in[i].wait()
         hi, loc = state_of(bt_v, x_v[:, lanes(q)] * e_wide)
         eex_v[:, lanes(q)] = hi
-        decx[q] = spread(q, 2 * NH, cols_b[ROWS - RW :, :])[RW - 1 :, :]
         for r in range(NZ):
             send1[0, r * NY + q] = loc[RW * r : RW * (r + 1), :]
         if i == 0:
@@ -219,12 +237,10 @@
         for dz in DZ_ORDER:
             if i or dz:
                 j = peer(i, dz)
+                to_seq(decx.at[0], decr.at[me], j, 2)
                 to_seq(send1.at[0, j], recv1.at[0, me], j, 0)
-        for dz in DZ_ORDER:
-            if i or dz:
-                j = peer(i, dz)
-                to_seq(decx.at[q], decr.at[me], j, 2)
-
+
+    c_in.wait()
     ct_hi, ct_lo = halves_of(c_ref[...].T)
     ct_v[0] = ct_hi
     ct_v[1] = ct_lo
@@ -232,7 +248,7 @@
     for i in range(NY):
         q = group(i)
         s_wide = spread(q, 2 * NH)
-        loads[NY + i].wait()
+        dy_in[i].wait()
         dy = jnp.where(row_live, dy_v[:, lanes(q)], 0.0)
         dy_v[:, lanes(q)] = dy
         hi, loc = state_of(ct_v, dy * s_wide)
@@ -246,11 +262,12 @@
     own = [
         pltpu.make_async_copy(send1.at[0, me], recv1.at[0, me], own_sem.at[0]),
         pltpu.make_async_copy(send1.at[1, me], recv1.at[1, me], own_sem.at[1]),
-        pltpu.make_async_copy(decx.at[my_y], decr.at[me], own_sem.at[2]),
+        pltpu.make_async_copy(decx.at[0], decr.at[me], own_sem.at[2]),
     ]
     for copy in own:
         copy.start()
 
+    prow_in.wait()
     bi = lax.broadcasted_iota(jnp.int32, (NB, NB), 0)
     bj = lax.broadcasted_iota(jnp.int32, (NB, NB), 1)
     par = jnp.broadcast_to(prow[...], (NB, NB))
@@ -341,38 +358,44 @@
     r_v[NB] = jnp.zeros((RW, QW), f32)
     settle(recv1.at[0, pl.ds(0, NB - 1)], recv_sem.at[0])
     settle(decr.at[pl.ds(0, NB - 1)], recv_sem.at[2])
+    mine = eh + (my_y * (NH // NY) + 2 * NH)
+    widen = jnp.where((er == mine) | (er == mine + NH), 1.0, 0.0).astype(bf16)
+    dec_rows = jnp.concatenate([decr[b] for b in range(NB)], axis=0).astype(bf16)
+    dec_wide = dot(dec_rows, widen)
+    for b in range(NB):
+        decw[b] = dec_wide[b : b + 1, :]
 
     def forward(b, carry):
         state = f_v[tab_s[b, 2]]
         send2[0, b] = state.astype(bf16)
-        f_v[b] = recv1[0, b].astype(f32) + decr[b] * state
+        f_v[b] = recv1[0, b].astype(f32) + decw[b] * state
         return carry
 
     def backward(k, carry):
         a = NB - 1 - k
         adj = r_v[tab_s[a, 0]]
         send2[1, a] = adj.astype(bf16)
-        r_v[a] = recv1[1, a].astype(f32) + decr[a] * adj + r_v[tab_s[a, 1]]
+        r_v[a] = recv1[1, a].astype(f32) + decw[a] * adj + r_v[tab_s[a, 1]]
         return carry
 
     def hand_back(w, k):
-        for dz in DZ_ORDER:
-            for i in range(NY):
+        for i in range(NY):
+            for dz in DZ_ORDER:
                 if i or dz:
                     j = peer(i, dz)
-                    to_seq(send2.at[w, j], recv2.at[w, me], j, k)
+                    to_seq(send2.at[w, j], recv2.at[w, me], j, k + i)
         copy = pltpu.make_async_copy(send2.at[w, me], recv2.at[w, me], own_sem.at[3 + w])
         copy.start()
         return copy
 
     lax.fori_loop(0, NB, forward, 0)
-    own_s = hand_back(0, 3)
+    own_s = hand_back(0, 9)
 
     lax.fori_loop(CUT1, CUT2, pair, 0)
 
     settle(recv1.at[1, pl.ds(0, NB - 1)], recv_sem.at[1])
     lax.fori_loop(0, NB, backward, 0)
-    own_g = hand_back(1, 4)
+    own_g = hand_back(1, 9 + NY)
 
     lax.fori_loop(CUT2, NH // 2, pair, 0)
 
@@ -384,8 +407,15 @@
     b_two = jnp.concatenate([b_hi, b_lo], axis=1)
     c_two = jnp.concatenate([c_hi, c_lo], axis=1)
 
-    def arrived(w, q):
-        return jnp.concatenate([recv2[w, r * NY + q] for r in range(NZ)], axis=0)
+    def arrived(w, i, own_part):
+        count = NZ if i else NZ - 1
+        if i == 0:
+            own_part.wait()
+        settle(recv2.at[w, pl.ds(0, count)], recv_sem.at[9 + NY * w + i])
+        return jnp.concatenate([recv2[w, r * NY + source(i)] for r in range(NZ)], axis=0)
+
+    def source(i):
+        return lax.rem(my_y + (NY - i), NY)
 
     def scatter(w, terms, k):
         part_v[w] = terms.astype(bf16)
@@ -409,11 +439,10 @@
         for d in (4, 3, 5, 2, 6, 1, 7):
             to_mp(out.at[share_of(mp), :], out.at[share_of(mp), :], lax.rem(mp + d, NMP), k + 1)
 
-    own_s.wait()
-    settle(recv2.at[0, pl.ds(0, NB - 1)], recv_sem.at[3])
-    s_in = [arrived(0, q) for q in range(NY)]
-    for q in range(NY):
-        dc = dc + dot_t(esdy_v[:, QW * q : QW * (q + 1)], s_in[q])
+    s_in = []
+    for i in range(NY):
+        s_in.append(arrived(0, i, own_s))
+        dc = dc + dot_t(esdy_v[:, lanes(source(i))], s_in[i])
     own_dc = scatter(0, dc, 5)
     acc = colq_v[...]
     sel_r = lax.broadcasted_iota(jnp.int32, (QW, TILE), 0) // WID
@@ -422,27 +451,27 @@
     def picks(q, base):
         return jnp.where(sel_l == sel_r + (q * (NH // NY) + base), 1.0, 0.0).astype(bf16)
 
-    for q in range(NY):
-        chi = dot(c_two, jnp.concatenate([s_in[q], s_in[q]], axis=0))
-        head = chi * esdy_v[:, QW * q : QW * (q + 1)].astype(f32)
-        acc = acc + dot(head.astype(bf16), picks(q, 0))
+    for i in range(NY):
+        chi = dot(c_two, jnp.concatenate([s_in[i], s_in[i]], axis=0))
+        head = chi * esdy_v[:, lanes(source(i))].astype(f32)
+        acc = acc + dot(head.astype(bf16), picks(source(i), 0))
     spread_share(0, dc_out, own_dc, 5)
 
-    own_g.wait()
-    settle(recv2.at[1, pl.ds(0, NB - 1)], recv_sem.at[4])
-    g_out = [arrived(1, q) for q in range(NY)]
-    for q in range(NY):
-        db = db + dot_t(eex_v[:, QW * q : QW * (q + 1)], g_out[q])
+    g_out = []
+    for i in range(NY):
+        g_out.append(arrived(1, i, own_g))
+        db = db + dot_t(eex_v[:, lanes(source(i))], g_out[i])
     own_db = scatter(1, db, 7)
 
     gs = jnp.zeros((8, NST), f32)
-    for q in range(NY):
-        span = slice(QW * q, QW * (q + 1))
-        bgo = dot(b_two, jnp.concatenate([g_out[q], g_out[q]], axis=0))
+    for i in range(NY):
+        q = source(i)
+        span = lanes(q)
+        bgo = dot(b_two, jnp.concatenate([g_out[i], g_out[i]], axis=0))
         dx_v[:, span] = dx_v[:, span] + eexp_v[:, span] * bgo
         eex = eex_v[:, span].astype(f32)
         acc = acc + dot((bgo * eex).astype(bf16), picks(q, NH))
-        both = jnp.sum(g_out[q].astype(f32) * s_in[q].astype(f32), axis=0, keepdims=True)
+        both = jnp.sum(g_out[i].astype(f32) * s_in[i].astype(f32), axis=0, keepdims=True)
         both_hi, both_lo = halves_of(jnp.broadcast_to(both, (8, QW)))
         gs = gs + dot(both_hi, picks(q, 0)) + dot(both_lo, picks(q, 0))
     flat = acc.T
@@ -462,8 +491,8 @@
     settle(send1.at[0, pl.ds(0, NB - 1)], send_sem.at[0])
     settle(send1.at[1, pl.ds(0, NB - 1)], send_sem.at[1])
     settle(decr.at[pl.ds(0, NB - 1)], send_sem.at[2])
-    settle(send2.at[0, pl.ds(0, NB - 1)], send_sem.at[3])
-    settle(send2.at[1, pl.ds(0, NB - 1)], send_sem.at[4])
+    for k in range(2 * NY):
+        settle(send2.at[0, pl.ds(0, NZ if k % NY else NZ - 1)], send_sem.at[9 + k])
     for w in range(2):
         settle(rbuf.at[w, pl.ds(0, NMP - 1)], send_sem.at[5 + 2 * w])
         settle(rbuf.at[w, pl.ds(0, NMP - 1)], send_sem.at[6 + 2 * w])
@@ -486,7 +515,6 @@
 
 def on_device(x_in, dy_out, b_in, c_in, log_decay, parents, lengths):
     vmem = pl.BlockSpec(memory_space=pltpu.VMEM)
-    smem = pl.BlockSpec(memory_space=pltpu.SMEM)
     anywhere = pl.BlockSpec(memory_space=pl.ANY)
     wide = (ROWS, CH)
     dma = pltpu.SemaphoreType.DMA
@@ -498,9 +526,14 @@
             pltpu.VMEM((ROWS, NST), bf16),
             pltpu.VMEM((NH, ROWS), f32),
         ),
-        in_specs=[smem, vmem, anywhere, anywhere, vmem, vmem, vmem],
+        in_specs=[anywhere] * 7,
         out_specs=(vmem, vmem, vmem, vmem),
         scratch_shapes=[
+            pltpu.SMEM((1, NB), jnp.int32),
+            pltpu.VMEM((1, NB), jnp.int32),
+            pltpu.VMEM((ROWS, NST), f32),
+            pltpu.VMEM((ROWS, NST), f32),
+            pltpu.VMEM((NH, ROWS), f32),
             pltpu.VMEM(wide, f32),
             pltpu.VMEM(wide, f32),
             pltpu.VMEM(wide, bf16),
@@ -519,7 +552,8 @@
             pltpu.SMEM((NB, TILE), jnp.int32),
             pltpu.VMEM((2, NB, RW, QW), bf16),
             pltpu.VMEM((2, NB, RW, QW), bf16),
-            pltpu.VMEM((NY, 1, QW), f32),
+            pltpu.VMEM((1, 1, NST), f32),
+            pltpu.VMEM((NB, 1, NST), f32),
             pltpu.VMEM((NB, 1, QW), f32),
             pltpu.VMEM((NB + 1, RW, QW), f32),
             pltpu.VMEM((NB + 1, RW, QW), f32),
@@ -527,16 +561,16 @@
             pltpu.VMEM((2, NB, RW, QW), bf16),
             pltpu.VMEM((2, ROWS, NST), bf16),
             pltpu.VMEM((2, NMP, SHARE, NST), bf16),
-            dma((2 * NY,)),
+            dma((2 * NY + 5,)),
             dma,
-            dma((9,)),
-            dma((9,)),
+            dma((9 + 2 * NY,)),
+            dma((9 + 2 * NY,)),
             dma((7,)),
         ],
         compiler_params=pltpu.CompilerParams(
             collective_id=0, has_side_effects=True, vmem_limit_bytes=52 * 1024 * 1024
         ),
-    )(lengths, parents.reshape(1, NB), x_in, dy_out, b_in, c_in, log_decay)
+    )(lengths.reshape(1, NB), parents.reshape(1, NB), x_in, dy_out, b_in, c_in, log_decay)
     return tuple(
         pl.pallas_call(
             finish,

time: 50.2 us -> 47.9 us (0.954)
  Pallas kernels: 49.5 us -> 47.2 us
    pallas_call x1, Pallas kernels: 48 us -> 45.7 us  [on_device(): pl.pallas_call(kernel, out_shape=(pltpu.VMEM(wide, f32), pltpu.VMEM((ROWS...]
where the time goes in v3:
time: 47.9 us; the launch traced here: 47.8 us
  Pallas kernels  47.2 us (99%)
  between operations  0.64 us (1%)
    pallas_call x1, Pallas kernels, on_device(): pl.pallas_call(kernel, out_shape=(pltpu.VMEM(wide, f32), pltpu.VMEM((ROWS...  45.7 us
    pallas_call x1, Pallas kernels, on_device(): pl.pallas_call(finish, out_shape=(jax.ShapeDtypeStruct(wide, f32), jax.Sh...  1.53 us

profile of v3, /device:TPU:1, one launch (start us, length us, event | category | flops | bytes accessed | tf_op | source)
XLA Modules:
  0.0 47.8 jit_solution(4902256521729141046)
XLA Ops:
  0.6 45.7 %shard_map.102 = (f32[512,1024]{1,0:T(8,128)S(1)}, bf16[512,128]{1,0:T(8,128)(2,1)S(1)}, bf16[512,128]{1,0:T(8,128)(2,1)S(1)}, f32[16,512]{1,0:T(8,128)S(1)}) custom-call(s32[1,32]{1,0:T(1,128)} %bitcast.2, s32[1,32]{1,0:T(1,128)} %bitcast.3, f32[512,1024]{1,0:T(8,128)} %x_hbm.1, f32[512,1024]{1,0:T(8,128)} %dy_hbm.1, f32[512,128]{1,0:T(8,128)} %b_hbm.1, ...), custom_call_target="tpu_custom_call" | custom-call | tf_op jit(solution)/shard_map/pallas_call | solution.py:521
  46.3 1.5 %shard_map.103 = (f32[512,1024]{1,0:T(8,128)}, f32[512,128]{1,0:T(8,128)}, f32[512,128]{1,0:T(8,128)}, f32[16,512]{1,0:T(8,128)}) custom-call(f32[512,1024]{1,0:T(8,128)S(1)} %get-tuple-element.8.xg_ref, bf16[512,128]{1,0:T(8,128)(2,1)S(1)} %get-tuple-element.9.db_ref, bf16[512,128]{1,0:T(8,128)(2,1)S(1)} %get-tuple-element.10.dc_ref, ...), custom_call_target="tpu_custom_call" | custom-call | tf_op jit(solution)/shard_map/pallas_call | solution.py:575

commit v4 on v3

--- a/solution.py
+++ b/solution.py
@@ -27,7 +27,7 @@
 RW = NST // NZ
 NMP = 8
 SHARE = ROWS // NMP
-CUT1, CUT2 = 3, 6
+CUT = 3
 DZ_ORDER = (4, 3, 5, 2, 6, 1, 7, 0)
 
 
@@ -113,6 +113,7 @@
     r_v,
     send2,
     recv2,
+    sum_v,
     part_v,
     rbuf,
     load_sem,
@@ -158,19 +159,6 @@
     def settle(like, sem):
         pltpu.make_async_copy(like, like, sem).wait()
 
-    loads = []
-
-    def load(src, dst):
-        copy = pltpu.make_async_copy(src, dst, load_sem.at[len(loads)])
-        copy.start()
-        loads.append(copy)
-        return copy
-
-    logd_in = load(logd_hbm, logd_ref)
-    lengths_in = load(lengths_hbm, lengths)
-    b_in = load(b_hbm, b_ref)
-    x_in = [load(x_hbm.at[:, lanes(group(i))], x_v.at[:, lanes(group(i))]) for i in range(NY)]
-
     barrier = pltpu.get_barrier_semaphore()
     for i in range(NY):
         for dz in DZ_ORDER:
@@ -178,6 +166,19 @@
                 pl.semaphore_signal(barrier, inc=1, device_id={"seq": peer(i, dz)}, device_id_type=MESH)
     for k in range(1, NMP):
         pl.semaphore_signal(barrier, inc=1, device_id={"mp": lax.rem(mp + k, NMP)}, device_id_type=MESH)
+
+    loads = []
+
+    def load(src, dst):
+        copy = pltpu.make_async_copy(src, dst, load_sem.at[len(loads)])
+        copy.start()
+        loads.append(copy)
+        return copy
+
+    logd_in = load(logd_hbm, logd_ref)
+    lengths_in = load(lengths_hbm, lengths)
+    b_in = load(b_hbm, b_ref)
+    x_in = [load(x_hbm.at[:, lanes(group(i))], x_v.at[:, lanes(group(i))]) for i in range(NY)]
 
     c_in = load(c_hbm, c_ref)
     dy_in = [load(dy_hbm.at[:, lanes(group(i))], dy_v.at[:, lanes(group(i))]) for i in range(NY)]
@@ -221,44 +222,64 @@
     def state_of(t_v, wide):
         hi, low = halves_of(wide)
         total = dot(t_v[0], hi) + dot(t_v[1], hi) + dot(t_v[0], low)
-        return hi, total.astype(bf16)
-
-    for i in range(NY):
+        return hi, low, total.astype(bf16)
+
+    def end_group(i, carry):
         q = group(i)
         e_wide = spread(q, 0)
         eexp_v[:, lanes(q)] = e_wide
-        x_in[i].wait()
-        hi, loc = state_of(bt_v, x_v[:, lanes(q)] * e_wide)
-        eex_v[:, lanes(q)] = hi
+        pltpu.make_async_copy(x_hbm.at[:, lanes(q)], x_v.at[:, lanes(q)], load_sem.at[3 + i]).wait()
+        hi, low, loc = state_of(bt_v, x_v[:, lanes(q)] * e_wide)
+        eex_v[0, :, lanes(q)] = hi
+        eex_v[1, :, lanes(q)] = low
         for r in range(NZ):
             send1[0, r * NY + q] = loc[RW * r : RW * (r + 1), :]
-        if i == 0:
+
+        @pl.when(i == 0)
+        def _():
             pl.semaphore_wait(barrier, NB - 1 + NMP - 1)
+
+        def away(dz):
+            j = peer(i, dz)
+            to_seq(decx.at[0], decr.at[me], j, 2)
+            to_seq(send1.at[0, j], recv1.at[0, me], j, 0)
+
         for dz in DZ_ORDER:
-            if i or dz:
-                j = peer(i, dz)
-                to_seq(decx.at[0], decr.at[me], j, 2)
-                to_seq(send1.at[0, j], recv1.at[0, me], j, 0)
+            if dz:
+                away(dz)
+        pl.when(i > 0)(lambda: away(0))
+        return carry
+
+    lax.fori_loop(0, NY, end_group, 0)
 
     c_in.wait()
     ct_hi, ct_lo = halves_of(c_ref[...].T)
     ct_v[0] = ct_hi
     ct_v[1] = ct_lo
     row_live = lax.broadcasted_iota(jnp.int32, (ROWS, QW), 0) < length
-    for i in range(NY):
+    def adj_group(i, carry):
         q = group(i)
         s_wide = spread(q, 2 * NH)
-        dy_in[i].wait()
+        pltpu.make_async_copy(dy_hbm.at[:, lanes(q)], dy_v.at[:, lanes(q)], load_sem.at[4 + NY + i]).wait()
         dy = jnp.where(row_live, dy_v[:, lanes(q)], 0.0)
         dy_v[:, lanes(q)] = dy
-        hi, loc = state_of(ct_v, dy * s_wide)
-        esdy_v[:, lanes(q)] = hi
+        hi, low, loc = state_of(ct_v, dy * s_wide)
+        esdy_v[0, :, lanes(q)] = hi
+        esdy_v[1, :, lanes(q)] = low
         for r in range(NZ):
             send1[1, r * NY + q] = loc[RW * r : RW * (r + 1), :]
+
+        def away(dz):
+            j = peer(i, dz)
+            to_seq(send1.at[1, j], recv1.at[1, me], j, 1)
+
         for dz in DZ_ORDER:
-            if i or dz:
-                j = peer(i, dz)
-                to_seq(send1.at[1, j], recv1.at[1, me], j, 1)
+            if dz:
+                away(dz)
+        pl.when(i > 0)(lambda: away(0))
+        return carry
+
+    lax.fori_loop(0, NY, adj_group, 0)
     own = [
         pltpu.make_async_copy(send1.at[0, me], recv1.at[0, me], own_sem.at[0]),
         pltpu.make_async_copy(send1.at[1, me], recv1.at[1, me], own_sem.at[1]),
@@ -349,21 +370,8 @@
             dx_v[us, span] = dx[jb]
         return carry
 
-    lax.fori_loop(0, CUT1, pair, 0)
-
-    tab.wait()
-    for copy in own:
-        copy.wait()
     f_v[NB] = jnp.zeros((RW, QW), f32)
     r_v[NB] = jnp.zeros((RW, QW), f32)
-    settle(recv1.at[0, pl.ds(0, NB - 1)], recv_sem.at[0])
-    settle(decr.at[pl.ds(0, NB - 1)], recv_sem.at[2])
-    mine = eh + (my_y * (NH // NY) + 2 * NH)
-    widen = jnp.where((er == mine) | (er == mine + NH), 1.0, 0.0).astype(bf16)
-    dec_rows = jnp.concatenate([decr[b] for b in range(NB)], axis=0).astype(bf16)
-    dec_wide = dot(dec_rows, widen)
-    for b in range(NB):
-        decw[b] = dec_wide[b : b + 1, :]
 
     def forward(b, carry):
         state = f_v[tab_s[b, 2]]
@@ -378,47 +386,84 @@
         r_v[a] = recv1[1, a].astype(f32) + decw[a] * adj + r_v[tab_s[a, 1]]
         return carry
 
+    def own2(w):
+        return pltpu.make_async_copy(send2.at[w, me], recv2.at[w, me], own_sem.at[3 + w])
+
     def hand_back(w, k):
-        for i in range(NY):
+        for i in range(NY - 1, -1, -1):
             for dz in DZ_ORDER:
                 if i or dz:
                     j = peer(i, dz)
                     to_seq(send2.at[w, j], recv2.at[w, me], j, k + i)
-        copy = pltpu.make_async_copy(send2.at[w, me], recv2.at[w, me], own_sem.at[3 + w])
-        copy.start()
-        return copy
-
-    lax.fori_loop(0, NB, forward, 0)
-    own_s = hand_back(0, 9)
-
-    lax.fori_loop(CUT1, CUT2, pair, 0)
-
-    settle(recv1.at[1, pl.ds(0, NB - 1)], recv_sem.at[1])
-    lax.fori_loop(0, NB, backward, 0)
-    own_g = hand_back(1, 9 + NY)
-
-    lax.fori_loop(CUT2, NH // 2, pair, 0)
+        own2(w).start()
+
+    def stage(g, carry):
+        lax.fori_loop(CUT * g, jnp.minimum(CUT * (g + 1), NH // 2), pair, 0)
+
+        @pl.when(g == 0)
+        def _():
+            tab.wait()
+            for copy in own:
+                copy.wait()
+            settle(recv1.at[0, pl.ds(0, NB - 1)], recv_sem.at[0])
+            settle(decr.at[pl.ds(0, NB - 1)], recv_sem.at[2])
+            mine = eh + (my_y * (NH // NY) + 2 * NH)
+            widen = jnp.where((er == mine) | (er == mine + NH), 1.0, 0.0).astype(bf16)
+            dec_rows = jnp.concatenate([decr[b] for b in range(NB)], axis=0).astype(bf16)
+            dec_wide = dot(dec_rows, widen)
+            for b in range(NB):
+                decw[b] = dec_wide[b : b + 1, :]
+            lax.fori_loop(0, NB, forward, 0)
+            hand_back(0, 9)
+
+        @pl.when(g == 1)
+        def _():
+            settle(recv1.at[1, pl.ds(0, NB - 1)], recv_sem.at[1])
+            lax.fori_loop(0, NB, backward, 0)
+            hand_back(1, 9 + NY)
+
+        return carry
+
+    lax.fori_loop(0, 3, stage, 0)
 
     b_hi, b_lo = halves_of(b_ref[...])
     c_hi, c_lo = halves_of(c_ref[...])
     mt_hi, mt_lo = halves_of(mt_v[...])
-    db = dot(mt_hi, c_hi) + dot(mt_lo, c_hi) + dot(mt_hi, c_lo)
-    dc = dot_0(mt_hi, b_hi) + dot_0(mt_lo, b_hi) + dot_0(mt_hi, b_lo)
+    sum_v[0] = dot_0(mt_hi, b_hi) + dot_0(mt_lo, b_hi) + dot_0(mt_hi, b_lo)
+    sum_v[1] = dot(mt_hi, c_hi) + dot(mt_lo, c_hi) + dot(mt_hi, c_lo)
     b_two = jnp.concatenate([b_hi, b_lo], axis=1)
     c_two = jnp.concatenate([c_hi, c_lo], axis=1)
 
-    def arrived(w, i, own_part):
-        count = NZ if i else NZ - 1
-        if i == 0:
-            own_part.wait()
-        settle(recv2.at[w, pl.ds(0, count)], recv_sem.at[9 + NY * w + i])
+    def returned(w, i):
         return jnp.concatenate([recv2[w, r * NY + source(i)] for r in range(NZ)], axis=0)
+
+    def gather(w, pair_v):
+        def column_group(k, carry):
+            i = NY - 1 - k
+
+            @pl.when(i > 0)
+            def _():
+                settle(recv2.at[w, pl.ds(0, NZ)], recv_sem.at[9 + NY * w + i])
+
+            @pl.when(i == 0)
+            def _():
+                own2(w).wait()
+                settle(recv2.at[w, pl.ds(0, NZ - 1)], recv_sem.at[9 + NY * w])
+
+            sum_v[w] += both_halves(pair_v, i, returned(w, i))
+            return carry
+
+        lax.fori_loop(0, NY, column_group, 0)
+
+    def both_halves(pair_v, i, state):
+        span = lanes(source(i))
+        return dot_t(pair_v[0, :, span], state) + dot_t(pair_v[1, :, span], state)
 
     def source(i):
         return lax.rem(my_y + (NY - i), NY)
 
-    def scatter(w, terms, k):
-        part_v[w] = terms.astype(bf16)
+    def scatter(w, k):
+        part_v[w] = sum_v[w].astype(bf16)
         for d in (4, 3, 5, 2, 6, 1, 7):
             to = lax.rem(mp + d, NMP)
             to_mp(part_v.at[w, share_of(to)], rbuf.at[w, mp], to, k)
@@ -439,42 +484,43 @@
         for d in (4, 3, 5, 2, 6, 1, 7):
             to_mp(out.at[share_of(mp), :], out.at[share_of(mp), :], lax.rem(mp + d, NMP), k + 1)
 
-    s_in = []
-    for i in range(NY):
-        s_in.append(arrived(0, i, own_s))
-        dc = dc + dot_t(esdy_v[:, lanes(source(i))], s_in[i])
-    own_dc = scatter(0, dc, 5)
-    acc = colq_v[...]
+    gather(0, esdy_v)
+    own_dc = scatter(0, 5)
     sel_r = lax.broadcasted_iota(jnp.int32, (QW, TILE), 0) // WID
     sel_l = lax.broadcasted_iota(jnp.int32, (QW, TILE), 1)
 
     def picks(q, base):
         return jnp.where(sel_l == sel_r + (q * (NH // NY) + base), 1.0, 0.0).astype(bf16)
 
-    for i in range(NY):
-        chi = dot(c_two, jnp.concatenate([s_in[i], s_in[i]], axis=0))
-        head = chi * esdy_v[:, lanes(source(i))].astype(f32)
-        acc = acc + dot(head.astype(bf16), picks(source(i), 0))
+    def head_terms(i, carry):
+        state = returned(0, i)
+        chi = dot(c_two, jnp.concatenate([state, state], axis=0))
+        head = chi * esdy_v[0, :, lanes(source(i))].astype(f32)
+        colq_v[...] += dot(head.astype(bf16), picks(source(i), 0))
+        return carry
+
+    lax.fori_loop(0, NY, head_terms, 0)
     spread_share(0, dc_out, own_dc, 5)
 
-    g_out = []
-    for i in range(NY):
-        g_out.append(arrived(1, i, own_g))
-        db = db + dot_t(eex_v[:, lanes(source(i))], g_out[i])
-    own_db = scatter(1, db, 7)
-
-    gs = jnp.zeros((8, NST), f32)
-    for i in range(NY):
+    gather(1, eex_v)
+    own_db = scatter(1, 7)
+
+    def tail_terms(i, gs):
         q = source(i)
         span = lanes(q)
-        bgo = dot(b_two, jnp.concatenate([g_out[i], g_out[i]], axis=0))
+        adj = returned(1, i)
+        bgo = dot(b_two, jnp.concatenate([adj, adj], axis=0))
         dx_v[:, span] = dx_v[:, span] + eexp_v[:, span] * bgo
-        eex = eex_v[:, span].astype(f32)
-        acc = acc + dot((bgo * eex).astype(bf16), picks(q, NH))
-        both = jnp.sum(g_out[i].astype(f32) * s_in[i].astype(f32), axis=0, keepdims=True)
+        eex = eex_v[0, :, span].astype(f32)
+        colq_v[...] += dot((bgo * eex).astype(bf16), picks(q, NH))
+        both = jnp.sum(adj.astype(f32) * returned(0, i).astype(f32), axis=0, keepdims=True)
         both_hi, both_lo = halves_of(jnp.broadcast_to(both, (8, QW)))
-        gs = gs + dot(both_hi, picks(q, 0)) + dot(both_lo, picks(q, 0))
-    flat = acc.T
+        return gs + dot(both_hi, picks(q, 0)) + dot(both_lo, picks(q, 0))
+
+    gs = lax.fori_loop(0, NY, tail_terms, jnp.zeros((8, NST), f32))
+    spread_share(1, db_out, own_db, 7)
+
+    flat = colq_v[...].T
     gs_col = gs.T[0:NH, 0:1]
     head = flat[0:NH]
     tail = flat[NH : 2 * NH]
@@ -485,8 +531,6 @@
     rowq = jnp.concatenate([rowq_v[h] for h in range(NH)], axis=0)
     total = running(rowq - colq + head, since, True) + running(tail, before, False) + dec * gs_col
     dl_ref[...] = jnp.where(live, total, 0.0)
-
-    spread_share(1, db_out, own_db, 7)
 
     settle(send1.at[0, pl.ds(0, NB - 1)], send_sem.at[0])
     settle(send1.at[1, pl.ds(0, NB - 1)], send_sem.at[1])
@@ -536,8 +580,8 @@
             pltpu.VMEM((NH, ROWS), f32),
             pltpu.VMEM(wide, f32),
             pltpu.VMEM(wide, f32),
-            pltpu.VMEM(wide, bf16),
-            pltpu.VMEM(wide, bf16),
+            pltpu.VMEM((2, *wide), bf16),
+            pltpu.VMEM((2, *wide), bf16),
             pltpu.VMEM(wide, f32),
             pltpu.VMEM((2, NST, ROWS), bf16),
             pltpu.VMEM((2, NST, ROWS), bf16),
@@ -559,6 +603,7 @@
             pltpu.VMEM((NB + 1, RW, QW), f32),
             pltpu.VMEM((2, NB, RW, QW), bf16),
             pltpu.VMEM((2, NB, RW, QW), bf16),
+            pltpu.VMEM((2, ROWS, NST), f32),
             pltpu.VMEM((2, ROWS, NST), bf16),
             pltpu.VMEM((2, NMP, SHARE, NST), bf16),
             dma((2 * NY + 5,)),

time: 47.9 us -> 47.7 us (level)
  no operation moved by 1% of the time
where the time goes in v4:
time: 47.7 us; the launch traced here: 47.6 us
  Pallas kernels  47 us (99%)
  between operations  0.64 us (1%)
    pallas_call x1, Pallas kernels, on_device(): pl.pallas_call(kernel, out_shape=(pltpu.VMEM(wide, f32), pltpu.VMEM((ROWS...  45.5 us
    pallas_call x1, Pallas kernels, on_device(): pl.pallas_call(finish, out_shape=(jax.ShapeDtypeStruct(wide, f32), jax.Sh...  1.53 us

profile of v4, /device:TPU:1, one launch (start us, length us, event | category | flops | bytes accessed | tf_op | source)
XLA Modules:
  0.0 47.6 jit_solution(6577478680051536965)
XLA Ops:
  0.6 45.5 %shard_map.102 = (f32[512,1024]{1,0:T(8,128)S(1)}, bf16[512,128]{1,0:T(8,128)(2,1)S(1)}, bf16[512,128]{1,0:T(8,128)(2,1)S(1)}, f32[16,512]{1,0:T(8,128)S(1)}) custom-call(s32[1,32]{1,0:T(1,128)} %bitcast.2, s32[1,32]{1,0:T(1,128)} %bitcast.3, f32[512,1024]{1,0:T(8,128)} %x_hbm.1, f32[512,1024]{1,0:T(8,128)} %dy_hbm.1, f32[512,128]{1,0:T(8,128)} %b_hbm.1, ...), custom_call_target="tpu_custom_call" | custom-call | tf_op jit(solution)/shard_map/pallas_call | solution.py:565
  46.1 1.5 %shard_map.103 = (f32[512,1024]{1,0:T(8,128)}, f32[512,128]{1,0:T(8,128)}, f32[512,128]{1,0:T(8,128)}, f32[16,512]{1,0:T(8,128)}) custom-call(f32[512,1024]{1,0:T(8,128)S(1)} %get-tuple-element.8.xg_ref, bf16[512,128]{1,0:T(8,128)(2,1)S(1)} %get-tuple-element.9.db_ref, bf16[512,128]{1,0:T(8,128)(2,1)S(1)} %get-tuple-element.10.dc_ref, ...), custom_call_target="tpu_custom_call" | custom-call | tf_op jit(solution)/shard_map/pallas_call | solution.py:620

commit v5 on v4

--- a/solution.py
+++ b/solution.py
@@ -457,7 +457,8 @@
 
     def both_halves(pair_v, i, state):
         span = lanes(source(i))
-        return dot_t(pair_v[0, :, span], state) + dot_t(pair_v[1, :, span], state)
+        both = jnp.concatenate([pair_v[0, :, span], pair_v[1, :, span]], axis=1)
+        return dot_t(both, jnp.concatenate([state, state], axis=1))
 
     def source(i):
         return lax.rem(my_y + (NY - i), NY)

time: 47.7 us -> 47.7 us (level)
  no operation moved by 1% of the time
where the time goes in v5:
time: 47.7 us; the launch traced here: 47.6 us
  Pallas kernels  47 us (99%)
  between operations  0.64 us (1%)
    pallas_call x1, Pallas kernels, on_device(): pl.pallas_call(kernel, out_shape=(pltpu.VMEM(wide, f32), pltpu.VMEM((ROWS...  45.5 us
    pallas_call x1, Pallas kernels, on_device(): pl.pallas_call(finish, out_shape=(jax.ShapeDtypeStruct(wide, f32), jax.Sh...  1.53 us

profile of v5, /device:TPU:1, one launch (start us, length us, event | category | flops | bytes accessed | tf_op | source)
XLA Modules:
  0.0 47.6 jit_solution(8366945247800878247)
XLA Ops:
  0.6 45.5 %shard_map.102 = (f32[512,1024]{1,0:T(8,128)S(1)}, bf16[512,128]{1,0:T(8,128)(2,1)S(1)}, bf16[512,128]{1,0:T(8,128)(2,1)S(1)}, f32[16,512]{1,0:T(8,128)S(1)}) custom-call(s32[1,32]{1,0:T(1,128)} %bitcast.2, s32[1,32]{1,0:T(1,128)} %bitcast.3, f32[512,1024]{1,0:T(8,128)} %x_hbm.1, f32[512,1024]{1,0:T(8,128)} %dy_hbm.1, f32[512,128]{1,0:T(8,128)} %b_hbm.1, ...), custom_call_target="tpu_custom_call" | custom-call | tf_op jit(solution)/shard_map/pallas_call | solution.py:566
  46.1 1.5 %shard_map.103 = (f32[512,1024]{1,0:T(8,128)}, f32[512,128]{1,0:T(8,128)}, f32[512,128]{1,0:T(8,128)}, f32[16,512]{1,0:T(8,128)}) custom-call(f32[512,1024]{1,0:T(8,128)S(1)} %get-tuple-element.8.xg_ref, bf16[512,128]{1,0:T(8,128)(2,1)S(1)} %get-tuple-element.9.db_ref, bf16[512,128]{1,0:T(8,128)(2,1)S(1)} %get-tuple-element.10.dc_ref, ...), custom_call_target="tpu_custom_call" | custom-call | tf_op jit(solution)/shard_map/pallas_call | solution.py:621
